TPU v7x, 32 devices: a whole 2x2x4 slice. The times are simulated.
32 devices in a mesh: fsdp: 32 (over z, y, x, core).
Axes of the slice: x: 2, y: 2, z: 4, core: 2. Of those that a mesh axis runs over, the one named last changes fastest.
Arguments:
- tokens: bfloat16 [12608, 768], P('fsdp'), may hold values from -6 to 6
- ln1_gain: bfloat16 [768], P('fsdp'), may hold values from 0.5 to 1.5
- ln1_shift: bfloat16 [768], P('fsdp'), may hold values from -3 to 3
- qkv_weight: bfloat16 [768, 2304], P('fsdp'), may hold values from -0.21875 to 0.21875
- qv_bias: bfloat16 [2, 768], P(None, 'fsdp'), may hold values from -3 to 3
- proj_weight: bfloat16 [768, 768], P('fsdp'), may hold values from -1 to 1
- proj_bias: bfloat16 [768], P('fsdp'), may hold values from -3 to 3
- ln2_gain: bfloat16 [768], P('fsdp'), may hold values from 0.5 to 1.5
- ln2_shift: bfloat16 [768], P('fsdp'), may hold values from -3 to 3
- router_weight: bfloat16 [768, 4], P('fsdp'), may hold values from -0.15625 to 0.15625
- expert_in: bfloat16 [3072, 4, 768], P('fsdp'), may hold values from -0.21875 to 0.21875
- expert_in_bias: bfloat16 [3072, 4], P('fsdp'), may hold values from -3 to 3
- expert_out: bfloat16 [3072, 4, 768], P('fsdp'), may hold values from -0.3125 to 0.3125
- expert_out_bias: bfloat16 [4, 768], P(None, 'fsdp'), may hold values from -3 to 3
- routes: int32 [12608, 2], P('fsdp'), may hold values from 0 to 3, all different within a row; in each aligned block of 394 rows (0 to 393, 394 to 787, ...) at most 246 rows name the same one
- out_grad: bfloat16 [12608, 768], P('fsdp'), may hold values from -6 to 6
Outputs:
- block_out: bfloat16 [12608, 768], P('fsdp')
- tokens_grad: float32 [12608, 768], P('fsdp')
- ln1_gain_grad: float32 [768], P('fsdp')
- ln1_shift_grad: float32 [768], P('fsdp')
- qkv_weight_grad: float32 [768, 2304], P('fsdp')
- qv_bias_grad: float32 [2, 768], P(None, 'fsdp')
- proj_weight_grad: float32 [768, 768], P('fsdp')
- proj_bias_grad: float32 [768], P('fsdp')
- ln2_gain_grad: float32 [768], P('fsdp')
- ln2_shift_grad: float32 [768], P('fsdp')
- router_weight_grad: float32 [768, 4], P('fsdp')
- expert_in_grad: float32 [3072, 4, 768], P('fsdp')
- expert_in_bias_grad: float32 [3072, 4], P('fsdp')
- expert_out_grad: float32 [3072, 4, 768], P('fsdp')
- expert_out_bias_grad: float32 [4, 768], P(None, 'fsdp')
Inputs may be any that keep to these rules, and one draw needn't show every extreme that they name: `routes`: each row names 2 different experts. Within the rows of one device no expert is named more than 246 times, and in some blocks one expert is named exactly 246 times.
All inputs are finite; a program needn't handle non-finite values.
Results may differ from a plain program's by a relative error of at most 0.015.
Values may be sent and summed in bfloat16 or wider, within the bound.
A program may use at most 320 MiB of HBM per device.

v0:
```python
import functools
import jax
import jax.numpy as jnp
from jax import lax
from jax.sharding import PartitionSpec as P

HEADS = 12
HD = 64
EXPERTS = 4
TOP = 2
LEN = 197
SEQ_DEV = 2
SLOTS = 256
SMALL_ROWS = 8


def layer_norm(values, gain_vec, shift_vec):
    row_mean = jnp.mean(values, axis=-1, keepdims=True)
    centred = values - row_mean
    spread = jnp.mean(centred * centred, axis=-1, keepdims=True)
    return centred * lax.rsqrt(spread + 1e-06) * gain_vec + shift_vec


def gelu_tanh(values):
    return jax.nn.gelu(values, approximate=True)


def take_rows(block, widths):
    pieces, at = ([], 0)
    for width in widths:
        pieces.append(block[:, at : at + width])
        at += width
    return pieces


def dot_f32(left, right, left_dim, right_dim):
    return lax.dot_general(
        left, right, (((left_dim,), (right_dim,)), ((), ())), preferred_element_type=jnp.float32
    )


def on_device(
    n_dev,
    tokens,
    ln1_gain,
    ln1_shift,
    qkv_weight,
    qv_bias,
    proj_weight,
    proj_bias,
    ln2_gain,
    ln2_shift,
    router_weight,
    expert_in,
    expert_in_bias,
    expert_out,
    expert_out_bias,
    routes,
    out_grad,
):
    highest = lax.Precision.HIGHEST
    f32 = jnp.float32
    low = jnp.bfloat16
    row_count, model_width = tokens.shape
    shape_four = (SEQ_DEV, LEN, HEADS, HD)
    query_scale = HD ** (-0.5)
    own = qkv_weight.shape[0]
    units = expert_in.shape[0]
    wide = 4 * model_width
    core = lax.axis_index("fsdp") % 2
    same_core = [list(range(c, n_dev, 2)) for c in range(2)]
    swap = [(i, i ^ 1) for i in range(n_dev)]
    small_parts = [
        ln1_gain,
        ln1_shift,
        qv_bias.reshape(-1),
        proj_bias,
        ln2_gain,
        ln2_shift,
        router_weight.T.reshape(-1),
        expert_out_bias.reshape(-1),
        expert_in_bias.T.reshape(-1),
    ]
    small_widths = [p.shape[0] for p in small_parts]
    small_total = sum(small_widths)
    small_mine = jnp.pad(
        jnp.concatenate(small_parts)[None, :], ((0, SMALL_ROWS - 1), (0, wide - small_total))
    )
    dense_mine = jnp.concatenate(
        [jnp.concatenate([qkv_weight, proj_weight], axis=1), small_mine], axis=0
    )
    dense = lax.all_gather(dense_mine, "fsdp", axis=0, tiled=True)
    dense = dense.reshape(n_dev, own + SMALL_ROWS, wide)
    w_in = lax.all_gather(
        expert_in.reshape(units, EXPERTS * model_width),
        "fsdp",
        axis=0,
        tiled=True,
        axis_index_groups=same_core,
    )
    w_out = lax.all_gather(
        expert_out.reshape(units, EXPERTS * model_width),
        "fsdp",
        axis=0,
        tiled=True,
        axis_index_groups=same_core,
    )
    weights = dense[:, :own, :].reshape(n_dev * own, wide)
    w_qkv = weights[:, : 3 * model_width]
    w_proj = weights[:, 3 * model_width :]
    gain1, shift1, bias_qv, bias_proj, gain2, shift2, w_router, bias_out, bias_in = take_rows(
        dense[:, own, :], small_widths
    )
    gain1 = gain1.reshape(-1).astype(f32)
    shift1 = shift1.reshape(-1).astype(f32)
    gain2 = gain2.reshape(-1).astype(f32)
    shift2 = shift2.reshape(-1).astype(f32)
    bias_proj = bias_proj.reshape(-1).astype(f32)
    bias_q = bias_qv[:, :own].reshape(-1).astype(f32)
    bias_v = bias_qv[:, own:].reshape(-1).astype(f32)
    w_router = jnp.stack([p.reshape(-1) for p in take_rows(w_router, [own] * EXPERTS)])
    bias_out = [p.reshape(-1).astype(f32) for p in take_rows(bias_out, [own] * EXPERTS)]
    bias_in = lax.dynamic_index_in_dim(
        bias_in.reshape(n_dev // 2, 2, EXPERTS * units), core, axis=1, keepdims=False
    )
    bias_in = [p.reshape(-1).astype(f32) for p in take_rows(bias_in, [units] * EXPERTS)]
    experts = jnp.arange(EXPERTS, dtype=jnp.int32)[None, :]
    pick = [(routes[:, j : j + 1] == experts).astype(f32) for j in range(TOP)]
    picked = pick[0] + pick[1]
    tri = jnp.arange(row_count)[:, None] > jnp.arange(row_count)[None, :]
    before = dot_f32(tri.astype(low), picked.astype(low), 1, 0)
    slot_ids = jnp.arange(EXPERTS * SLOTS, dtype=jnp.int32)[None, :]
    hit = []
    for j in range(TOP):
        slot = jnp.sum(pick[j] * before, axis=1, keepdims=True).astype(jnp.int32)
        hit.append(slot_ids == routes[:, j : j + 1] * SLOTS + slot)
    dispatch = (hit[0] | hit[1]).astype(low)
    inputs = tokens.astype(f32)
    normed_full, norm1_pull = jax.vjp(layer_norm, inputs, gain1, shift1)
    normed = normed_full.astype(low)
    projected = jnp.dot(normed, w_qkv, preferred_element_type=f32)
    queries = ((projected[:, :model_width] + bias_q) * query_scale).astype(low).reshape(shape_four)
    key_rows = projected[:, model_width : 2 * model_width].astype(low).reshape(shape_four)
    values = (projected[:, 2 * model_width :] + bias_v).astype(low).reshape(shape_four)
    scores = jnp.einsum("sqhd,skhd->shqk", queries, key_rows, preferred_element_type=f32)
    exp_scores = jnp.exp(scores - jnp.max(scores, axis=-1, keepdims=True))
    probs_full = exp_scores / jnp.sum(exp_scores, axis=-1, keepdims=True)
    probs_low = probs_full.astype(low)
    attended = jnp.einsum("shqk,skhd->sqhd", probs_low, values, preferred_element_type=f32)
    attended = attended.reshape(row_count, model_width).astype(low)
    middle = inputs + jnp.dot(attended, w_proj, preferred_element_type=f32) + bias_proj
    normed2_full, norm2_pull = jax.vjp(layer_norm, middle, gain2, shift2)
    normed2 = normed2_full.astype(low)
    gate_probs = jax.nn.softmax(dot_f32(normed2, w_router, 1, 1), axis=-1)
    chosen = [jnp.sum(gate_probs * pick[j], axis=1, keepdims=True) for j in range(TOP)]
    combine = (jnp.where(hit[0], chosen[0], 0.0) + jnp.where(hit[1], chosen[1], 0.0)).astype(low)

    def pair_rows(mine):
        mine = mine.reshape(EXPERTS, SLOTS, model_width)
        theirs = lax.ppermute(mine, "fsdp", swap)
        return [jnp.concatenate([mine[e], theirs[e]], axis=0) for e in range(EXPERTS)]

    def pair_sum(partial):
        sent = jnp.stack([p[SLOTS:].astype(low) for p in partial])
        got = lax.ppermute(sent, "fsdp", swap)
        return [p[:SLOTS] + got[e].astype(f32) for e, p in enumerate(partial)]

    slot_rows = pair_rows(dot_f32(dispatch, normed2, 0, 0).astype(low))
    grad_result_mine = dot_f32(combine, out_grad, 0, 0).astype(low)
    grad_result = pair_rows(grad_result_mine)

    def expert(weight, e):
        return weight[:, e * model_width : (e + 1) * model_width]

    def scatter_units(terms):
        return lax.psum_scatter(
            terms, "fsdp", scatter_dimension=0, tiled=True, axis_index_groups=same_core
        )

    each = range(EXPERTS)
    pre_act = [dot_f32(slot_rows[e], expert(w_in, e), 1, 1) + bias_in[e] for e in each]
    hidden, pulls = ([], [])
    for e in each:
        out, pull = jax.vjp(gelu_tanh, pre_act[e])
        hidden.append(out.astype(low))
        pulls.append(pull)
    out_terms = [dot_f32(hidden[e], grad_result[e], 0, 0).astype(low) for e in each]
    out_terms = jnp.concatenate(out_terms, axis=1)
    grad_pre = [
        pulls[e](dot_f32(grad_result[e], expert(w_out, e), 1, 1))[0].astype(low) for e in each
    ]
    in_terms = [dot_f32(grad_pre[e], slot_rows[e], 0, 0).astype(low) for e in each]
    in_terms = jnp.concatenate(in_terms, axis=1)
    out_terms, in_terms, hidden, grad_pre = lax.optimization_barrier(
        (out_terms, in_terms, hidden, grad_pre)
    )
    expert_out_mine = scatter_units(out_terms)
    expert_in_mine = scatter_units(in_terms)
    grad_bias_in = jnp.stack([jnp.sum(grad_pre[e].astype(f32), axis=0) for e in each])
    summed = pair_sum([dot_f32(hidden[e], expert(w_out, e), 1, 0) for e in each])
    result = jnp.concatenate([(summed[e] + bias_out[e]).astype(low) for e in each], axis=0)
    grad_slots = pair_sum([dot_f32(grad_pre[e], expert(w_in, e), 1, 0) for e in each])
    grad_slots = jnp.concatenate([g.astype(low) for g in grad_slots], axis=0)
    block_out = (middle + jnp.dot(combine, result, preferred_element_type=f32)).astype(low)
    grad_top = out_grad.astype(f32)
    slot_dots = dot_f32(out_grad, result, 1, 1) * dispatch.astype(f32)
    grad_gates = jnp.concatenate(
        [jnp.sum(slot_dots[:, e * SLOTS : (e + 1) * SLOTS], axis=1, keepdims=True) for e in each],
        axis=1,
    )
    grad_logits = gate_probs * (
        grad_gates - jnp.sum(gate_probs * grad_gates, axis=-1, keepdims=True)
    )
    grad_router = jnp.dot(grad_logits.T, normed2.astype(f32), precision=highest)
    grad_normed2 = jnp.dot(grad_logits, w_router.astype(f32), precision=highest)
    grad_normed2 = grad_normed2 + jnp.dot(dispatch, grad_slots, preferred_element_type=f32)
    grad_mid_norm, grad_gain2, grad_shift2 = norm2_pull(grad_normed2)
    grad_middle = grad_top + grad_mid_norm
    grad_branch = grad_middle.astype(low)
    grad_bias_proj = jnp.sum(grad_branch.astype(f32), axis=0)
    grad_proj = dot_f32(attended, grad_branch, 0, 0)
    grad_attended = dot_f32(grad_branch, w_proj, 1, 1).astype(low).reshape(shape_four)
    grad_probs = jnp.einsum("sqhd,skhd->shqk", grad_attended, values, preferred_element_type=f32)
    grad_values = jnp.einsum(
        "shqk,sqhd->skhd", probs_low, grad_attended, preferred_element_type=f32
    ).astype(low)
    grad_scores = (
        probs_full * (grad_probs - jnp.sum(probs_full * grad_probs, axis=-1, keepdims=True))
    ).astype(low)
    grad_queries = jnp.einsum(
        "shqk,skhd->sqhd", grad_scores, key_rows, preferred_element_type=f32
    ).astype(low)
    grad_keys = jnp.einsum(
        "shqk,sqhd->skhd", grad_scores, queries, preferred_element_type=f32
    ).astype(low)
    grad_query_pre = grad_queries.astype(f32).reshape(row_count, model_width) * query_scale
    grad_values = grad_values.reshape(row_count, model_width)
    grad_projected = jnp.concatenate(
        [grad_query_pre.astype(low), grad_keys.reshape(row_count, model_width), grad_values], axis=1
    )
    grad_qkv = dot_f32(normed, grad_projected, 0, 0)
    grad_normed = dot_f32(grad_projected, w_qkv, 1, 1)
    grad_in_norm, grad_gain1, grad_shift1 = norm1_pull(grad_normed)
    tokens_grad = grad_middle + grad_in_norm

    def by_owner(rows):
        return (
            rows.reshape(-1, n_dev, rows.shape[-1] // n_dev).transpose(1, 0, 2).reshape(n_dev, -1)
        )

    here = (jnp.arange(2) == core).astype(f32)
    bias_in_slots = grad_bias_in.reshape(EXPERTS, n_dev // 2, 1, units) * here[None, None, :, None]
    grad_bias_out = jnp.sum(
        grad_result_mine.astype(f32).reshape(EXPERTS, SLOTS, model_width), axis=1
    )
    small_grads = jnp.concatenate(
        [
            by_owner(
                jnp.concatenate(
                    [
                        jnp.stack(
                            [
                                grad_gain1,
                                grad_shift1,
                                jnp.sum(grad_query_pre, axis=0),
                                jnp.sum(grad_values.astype(f32), axis=0),
                                grad_bias_proj,
                                grad_gain2,
                                grad_shift2,
                            ]
                        ),
                        grad_router,
                        grad_bias_out,
                    ],
                    axis=0,
                )
            ),
            by_owner(bias_in_slots.reshape(EXPERTS, n_dev * units)),
        ],
        axis=1,
    ).astype(low)
    small_grads = jnp.pad(
        small_grads[:, None, :], ((0, 0), (0, SMALL_ROWS - 1), (0, wide - small_total))
    )
    dense_grads = jnp.concatenate([grad_qkv.astype(low), grad_proj.astype(low)], axis=1)
    dense_grads = jnp.concatenate([dense_grads.reshape(n_dev, own, wide), small_grads], axis=1)
    dense_grads, expert_out_mine, expert_in_mine = lax.optimization_barrier(
        (dense_grads, expert_out_mine, expert_in_mine)
    )
    dense_out = lax.psum_scatter(
        dense_grads.reshape(n_dev * (own + SMALL_ROWS), wide),
        "fsdp",
        scatter_dimension=0,
        tiled=True,
    ).astype(f32)
    small = [p[0] for p in take_rows(dense_out[own : own + 1], small_widths)]
    expert_shape = (units, EXPERTS, model_width)
    return (
        block_out,
        tokens_grad,
        small[0],
        small[1],
        dense_out[:own, : 3 * model_width],
        small[2].reshape(2, own),
        dense_out[:own, 3 * model_width :],
        small[3],
        small[4],
        small[5],
        small[6].reshape(EXPERTS, own).T,
        expert_in_mine.astype(f32).reshape(expert_shape),
        small[8].reshape(EXPERTS, units).T,
        expert_out_mine.astype(f32).reshape(expert_shape),
        small[7].reshape(EXPERTS, own),
    )


def solution(mesh):
    in_specs = (
        P("fsdp", None),
        P("fsdp"),
        P("fsdp"),
        P("fsdp", None),
        P(None, "fsdp"),
        P("fsdp", None),
        P("fsdp"),
        P("fsdp"),
        P("fsdp"),
        P("fsdp", None),
        P("fsdp", None, None),
        P("fsdp", None),
        P("fsdp", None, None),
        P(None, "fsdp"),
        P("fsdp", None),
        P("fsdp", None),
    )
    out_specs = (
        P("fsdp", None),
        P("fsdp", None),
        P("fsdp"),
        P("fsdp"),
        P("fsdp", None),
        P(None, "fsdp"),
        P("fsdp", None),
        P("fsdp"),
        P("fsdp"),
        P("fsdp"),
        P("fsdp", None),
        P("fsdp", None, None),
        P("fsdp", None),
        P("fsdp", None, None),
        P(None, "fsdp"),
    )
    return jax.shard_map(
        functools.partial(on_device, mesh.shape["fsdp"]),
        mesh=mesh,
        in_specs=in_specs,
        out_specs=out_specs,
        check_vma=False,
    )
```

profile of v0, /device:TPU:0, one launch (start us, length us, event | category | flops | bytes accessed | tf_op | source)
XLA Modules:
  0.0 876.5 jit_solution(18161666276513297244)
XLA Ops:
  19.7 68.1 %all-gather.4.cloned.1.call-done = bf16[1024,3072]{1,0:T(8,128)(2,1)} async-done(((bf16[32,3072]{1,0:T(8,128)(2,1)}), bf16[1024,3072]{1,0:T(8,128)(2,1)}) %all-gather.4.cloned.1.call-update) | async-done | bytes 6291472 | tf_op jit(solution)/shard_map/all_gather | solution.py:92
  89.4 4.8 slice.421
  99.1 3.8 fusion.33
  117.1 3.8 fusion.179
  146.9 65.3 %all-gather.6.cloned.1.call-done = bf16[1536,3072]{1,0:T(8,128)(2,1)} async-done(((bf16[96,3072]{1,0:T(8,128)(2,1)}), bf16[1536,3072]{1,0:T(8,128)(2,1)}) %all-gather.6.cloned.1.call-update) | async-done | bytes 9437200 | tf_op jit(solution)/shard_map/all_gather | solution.py:94
  212.2 5.7 multiply_convert_fusion.4
  221.9 113.8 %all-gather.8.cloned.1.call-done = bf16[1536,3072]{1,0:T(8,128)(2,1)} async-done(((bf16[96,3072]{1,0:T(8,128)(2,1)}), bf16[1536,3072]{1,0:T(8,128)(2,1)}) %all-gather.8.cloned.1.call-update) | async-done | bytes 9437200 | tf_op jit(solution)/shard_map/all_gather | solution.py:101
  335.6 6.2 fusion.9
  343.6 3.7 multiply_convert_fusion.1
  348.9 4.9 fusion.30
  359.3 4.6 fusion.23
  369.0 4.6 fusion.16
  375.9 4.4 pad_maximum_fusion
  380.2 4.3 pad_maximum_fusion.1
  384.5 12.6 %copy.130 = bf16[1536,3072]{1,0:T(8,128)(2,1)} copy(bf16[1536,3072]{0,1:T(8,128)(2,1)} %pad_maximum_fusion) | data formatting | bytes 18874368
  397.2 12.7 %copy.132 = bf16[1536,3072]{1,0:T(8,128)(2,1)} copy(bf16[1536,3072]{0,1:T(8,128)(2,1)} %pad_maximum_fusion.1) | data formatting | bytes 18874368
  411.1 3.7 fusion.53
  414.8 4.2 fusion.47
  436.2 3.6 fusion.65
  466.8 3.4 multiply_reduce_fusion
  486.2 5.1 fusion.171
  501.3 65.2 %reduce-scatter.10.cloned.1.call-done = bf16[96,3072]{1,0:T(8,128)(2,1)} async-done(((bf16[1536,3072]{1,0:T(8,128)(2,1)}), bf16[96,3072]{1,0:T(8,128)(2,1)}) %reduce-scatter.10.cloned.1.call-update) | async-done | bytes 589840
  568.8 174.5 %reduce-scatter.12.cloned.1.call-done = bf16[96,3072]{1,0:T(8,128)(2,1)} async-done(((bf16[1536,3072]{1,0:T(8,128)(2,1)}), bf16[96,3072]{1,0:T(8,128)(2,1)}) %reduce-scatter.12.cloned.1.call-update) | async-done | bytes 589840
  754.2 107.9 %reduce-scatter.8.cloned.1.call-done = bf16[32,3072]{1,0:T(8,128)(2,1)} async-done(((bf16[1024,3072]{1,0:T(8,128)(2,1)}), bf16[32,3072]{1,0:T(8,128)(2,1)}) %reduce-scatter.8.cloned.1.call-update) | async-done | bytes 196624 | tf_op jit(solution)/shard_map/reduce_scatter | solution.py:290
  (433 shorter events, 169.2 us)
Async XLA Ops:
  7.2 10.3 %copy-start.37 = (bf16[96,4,768]{2,1,0:T(4,128)(2,1)S(1)}, bf16[96,4,768]{2,1,0:T(4,128)(2,1)}, u32[]{:S(2)}) copy-start(bf16[96,4,768]{2,1,0:T(4,128)(2,1)} %param.28) | copy-start | bytes 1769476
  7.2 11.3 %copy-start.4 = (bf16[394,768]{1,0:T(8,128)(2,1)S(1)}, bf16[394,768]{1,0:T(8,128)(2,1)}, u32[]{:S(2)}) copy-start(bf16[394,768]{1,0:T(8,128)(2,1)} %param.16) | copy-start | bytes 1815556
  7.2 80.6 %all-gather.4.cloned.1.call-start = ((), (), s32[]{:S(2)}) async-start(), calls=%async_computation.3 | async-start | bytes 6488064 | tf_op jit(solution)/shard_map/all_gather | solution.py:92
  15.4 196.7 %all-gather.6.cloned.1.call-start = ((), (), s32[]{:S(2)}) async-start(), calls=%async_computation.4 | async-start | bytes 10027008 | tf_op jit(solution)/shard_map/all_gather | solution.py:94
  17.5 318.2 %all-gather.8.cloned.1.call-start = ((), (), s32[]{:S(2)}) async-start(), calls=%async_computation.5 | async-start | bytes 10027008 | tf_op jit(solution)/shard_map/all_gather | solution.py:101
  18.5 548.1 %reduce-scatter.10.cloned.1.call-start = ((), (), s32[]{:S(2)}) async-start(), calls=%async_computation.7 | async-start | bytes 10027008
  18.7 80.3 %copy-start.71 = (f32[394]{0:T(512)}, f32[394]{0:T(512)S(1)}, u32[]{:S(2)}) copy-start(f32[394]{0:T(512)S(1)} %broadcast_multiply_fusion.1) | copy-start | bytes 4732
  19.0 75.2 %copy-start.81 = (f32[394]{0:T(512)}, f32[394]{0:T(512)S(1)}, u32[]{:S(2)}) copy-start(f32[394]{0:T(512)S(1)} %fusion.96) | copy-start | bytes 4732
  19.1 80.0 %copy-start.85 = (f32[394]{0:T(512)}, f32[394]{0:T(512)S(1)}, u32[]{:S(2)}) copy-start(f32[394]{0:T(512)S(1)} %fusion.144) | copy-start | bytes 4732
  95.8 33.6 %copy-start.73 = (bf16[1,768]{1,0:T(2,128)(2,1)}, bf16[1,768]{1,0:T(2,128)(2,1)S(1)}, u32[]{:S(2)}) copy-start(bf16[1,768]{1,0:T(2,128)(2,1)S(1)} %stack_reshape.15) | copy-start | bytes 4612
  98.0 30.5 %copy-start.63 = (f32[768]{0:T(1024)}, f32[768]{0:T(1024)S(1)}, u32[]{:S(2)}) copy-start(f32[768]{0:T(1024)S(1)} %reshape.457) | copy-start | bytes 9220
  107.0 10.1 %copy-start.8 = (bf16[2,197,12,64]{1,3,2,0:T(8,128)(2,1)}, bf16[2,197,12,64]{1,3,2,0:T(8,128)(2,1)S(1)}, u32[]{:S(2)}) copy-start(bf16[2,197,12,64]{1,3,2,0:T(8,128)(2,1)S(1)} %copy.102) | copy-start | bytes 1815556
  112.5 8.3 copy-start.6
  128.1 326.3 %copy-start = (f32[394,768]{1,0:T(8,128)}, f32[394,768]{1,0:T(8,128)S(1)}, u32[]{:S(2)}) copy-start(f32[394,768]{1,0:T(8,128)S(1)} %get-tuple-element.184) | copy-start | bytes 3631108
  130.0 321.8 %copy-start.92 = (s32[394,1]{0,1:T(1,128)}, s32[394,1]{0,1:T(1,128)S(1)}, u32[]{:S(2)}) copy-start(s32[394,1]{0,1:T(1,128)S(1)} %get-tuple-element.177) | copy-start | bytes 4732
  130.0 321.8 %copy-start.94 = (s32[394,1]{0,1:T(1,128)}, s32[394,1]{0,1:T(1,128)S(1)}, u32[]{:S(2)}) copy-start(s32[394,1]{0,1:T(1,128)S(1)} %get-tuple-element.178) | copy-start | bytes 4732
  132.6 9.2 %collective-permute-start.1 = (bf16[4,256,768]{2,1,0:T(8,128)(2,1)}, bf16[4,256,768]{2,1,0:T(8,128)(2,1)}, u32[]{:S(2)}, u32[]{:S(2)}) collective-permute-start(bf16[4,256,768]{2,1,0:T(8,128)(2,1)} %bitcast.14), channel_id=1, source_target_pairs={{0,1},{1,0},{2,3},{3,2},{4,5},{5,4},{6,7},{7,6},{8,9},{9,8},{10,11... | collective-permute-start | bytes 4718600 | tf_op jit(solution)/shard_map/ppermute | solution.py:160
  135.4 8.9 %collective-permute-start = (bf16[4,256,768]{2,1,0:T(8,128)(2,1)}, bf16[4,256,768]{2,1,0:T(8,128)(2,1)}, u32[]{:S(2)}, u32[]{:S(2)}) collective-permute-start(bf16[4,256,768]{2,1,0:T(8,128)(2,1)} %bitcast.11), channel_id=1, source_target_pairs={{0,1},{1,0},{2,3},{3,2},{4,5},{5,4},{6,7},{7,6},{8,9},{9,8},{10,11... | collective-permute-start | bytes 4718600 | tf_op jit(solution)/shard_map/ppermute | solution.py:160
  397.2 346.1 %reduce-scatter.12.cloned.1.call-start = ((), (), s32[]{:S(2)}) async-start(), calls=%async_computation.8 | async-start | bytes 10027008
  409.9 452.1 %reduce-scatter.8.cloned.1.call-start = ((), (), s32[]{:S(2)}) async-start(), calls=%async_computation.6 | async-start | bytes 6488064 | tf_op jit(solution)/shard_map/reduce_scatter | solution.py:290
  411.1 8.1 slice-start.6
  411.1 8.1 slice-start.7
  424.2 19.7 %collective-permute-start.2 = (bf16[4,256,768]{2,1,0:T(8,128)(2,1)}, bf16[4,256,768]{2,1,0:T(8,128)(2,1)}, u32[]{:S(2)}, u32[]{:S(2)}) collective-permute-start(bf16[4,256,768]{2,1,0:T(8,128)(2,1)} %pad_maximum_fusion.3), channel_id=1, source_target_pairs={{0,1},{1,0},{2,3},{3,2},{4,5},{5,4},{6,7},{7,6},{8,9},{9,8},{10,11... | collective-permute-start | bytes 4718600 | tf_op jit(solution)/shard_map/ppermute | solution.py:165
  443.0 6.1 collective-permute-start.3
  (103 other events, 280.2 us)
Sparse Core Ops, SparseCore 0:
  15.5 72.1 all-gather.3
  91.2 120.9 all-gather.5
  215.0 120.6 all-gather.7
  397.3 169.2 reduce-scatter.9
  573.0 170.2 reduce-scatter.11
  748.8 113.1 reduce-scatter.7
where the time goes:
time: 884 us; the launch traced here: 877 us
  waiting for transfers between devices  595 us (67%)
  local copies, waits for them, and re-layouts  114 us (13%)
  matrix products  114 us (13%)
  other arithmetic  36 us (4%)
  between operations  16.4 us (2%)
    unnamed x8, waiting for transfers between devices  240 us
    all_gather x1, waiting for transfers between devices, on_device(): lax.all_gather(expert_out.reshape(units, EXPERTS * model_width), 'fsdp',...  114 us
    reduce_scatter x1, waiting for transfers between devices, on_device(): lax.psum_scatter(dense_grads.reshape(n_dev * (own + SMALL_ROWS), wide), '...  108 us
    dot_general x33, matrix products, dot_f32(): lax.dot_general(left, right, (((left_dim,), (right_dim,)), ((), ())), pre...  87.3 us
    all_gather x1, waiting for transfers between devices, on_device(): dense = lax.all_gather(dense_mine, 'fsdp', axis=0, tiled=True)  68.1 us
    all_gather x1, waiting for transfers between devices, on_device(): lax.all_gather(expert_in.reshape(units, EXPERTS * model_width), 'fsdp', a...  65.3 us
    unnamed x253, local copies, waits for them, and re-layouts  43 us
  transfers between devices with their start and end apart: 10, of which 6 were waited for; matrix products, arithmetic and copies ran while one was open for 20% of the time, Pallas kernels for 0%

commit v1 on v0

--- a/solution.py
+++ b/solution.py
@@ -89,7 +89,15 @@
     dense_mine = jnp.concatenate(
         [jnp.concatenate([qkv_weight, proj_weight], axis=1), small_mine], axis=0
     )
-    dense = lax.all_gather(dense_mine, "fsdp", axis=0, tiled=True)
+    ways, here_2 = (lax.axis_size("fsdp"), lax.axis_index("fsdp"))
+    grown, reach = (dense_mine, 1)
+    while reach < ways:
+        theirs_2 = lax.ppermute(grown, "fsdp", [(d, d ^ reach) for d in range(ways)])
+        mine_first = jnp.concatenate([grown, theirs_2], axis=0)
+        theirs_first = jnp.concatenate([theirs_2, grown], axis=0)
+        grown = jnp.where(here_2 & reach == 0, mine_first, theirs_first)
+        reach = 2 * reach
+    dense = grown
     dense = dense.reshape(n_dev, own + SMALL_ROWS, wide)
     w_in = lax.all_gather(
         expert_in.reshape(units, EXPERTS * model_width),

time: 884 us -> 949 us (1.074)
  waiting for transfers between devices: 595 us -> 652 us
  local copies, waits for them, and re-layouts: 114 us -> 104 us
  other arithmetic: 36 us -> 45.5 us
    ppermute x0 -> x5, waiting for transfers between devices: none -> 277 us  [on_device(): lax.ppermute(grown, 'fsdp', [(d, d ^ reach) for d in range(ways)])]
    all_gather x1, waiting for transfers between devices: 114 us -> 27.5 us  [on_device(): lax.all_gather(expert_out.reshape(units, EXPERTS * model_width), 'fsdp',...]
    all_gather x1 -> x0, waiting for transfers between devices: 68.1 us -> none  [on_device(): dense = lax.all_gather(dense_mine, 'fsdp', axis=0, tiled=True)]
    all_gather x1, waiting for transfers between devices: 65.3 us -> 0.01 us  [on_device(): lax.all_gather(expert_in.reshape(units, EXPERTS * model_width), 'fsdp', a...]
    select_n x0 -> x5, other arithmetic: none -> 9.73 us  [on_device(): grown = jnp.where(here_2 & reach == 0, mine_first, theirs_first)]
    unnamed x8 -> x7, waiting for transfers between devices: 240 us -> 239 us
    unnamed x253 -> x288, local copies, waits for them, and re-layouts: 43 us -> 42.9 us
  transfers between devices with their start and end apart: 10 -> 14, of which waited for: 6 -> 9; matrix products, arithmetic and copies ran while one was open for 20% -> 19% of each run, Pallas kernels for 0% -> 0%
where the time goes in v1:
time: 949 us; the launch traced here: 939 us
  waiting for transfers between devices  652 us (69%)
  matrix products  114 us (12%)
  local copies, waits for them, and re-layouts  104 us (11%)
  other arithmetic  45.5 us (5%)
  between operations  16.4 us (2%)
    ppermute x5, waiting for transfers between devices, on_device(): lax.ppermute(grown, 'fsdp', [(d, d ^ reach) for d in range(ways)])  277 us
    unnamed x7, waiting for transfers between devices  239 us
    reduce_scatter x1, waiting for transfers between devices, on_device(): lax.psum_scatter(dense_grads.reshape(n_dev * (own + SMALL_ROWS), wide), '...  108 us
    dot_general x33, matrix products, dot_f32(): lax.dot_general(left, right, (((left_dim,), (right_dim,)), ((), ())), pre...  87.3 us
    unnamed x288, local copies, waits for them, and re-layouts  42.9 us
    all_gather x1, waiting for transfers between devices, on_device(): lax.all_gather(expert_out.reshape(units, EXPERTS * model_width), 'fsdp',...  27.5 us
  transfers between devices with their start and end apart: 14, of which 9 were waited for; matrix products, arithmetic and copies ran while one was open for 19% of the time, Pallas kernels for 0%

profile of v1, /device:TPU:0, one launch (start us, length us, event | category | flops | bytes accessed | tf_op | source)
XLA Modules:
  0.0 939.5 jit_solution(14971593964026752716)
XLA Ops:
  16.6 11.3 %collective-permute-done.1 = bf16[64,3072]{1,0:T(8,128)(2,1)S(1)} collective-permute-done((bf16[64,3072]{1,0:T(8,128)(2,1)S(1)}, bf16[64,3072]{1,0:T(8,128)(2,1)S(1)}, u32[]{:S(2)}, u32[]{:S(2)}) %collective-permute-start.1) | collective-permute-done | bytes 393248 | tf_op jit(solution)/shard_map/ppermute | solution.py:95
  29.5 17.3 %collective-permute-done.2 = bf16[128,3072]{1,0:T(8,128)(2,1)S(1)} collective-permute-done((bf16[128,3072]{1,0:T(8,128)(2,1)S(1)}, bf16[128,3072]{1,0:T(8,128)(2,1)S(1)}, u32[]{:S(2)}, u32[]{:S(2)}) %collective-permute-start.2) | collective-permute-done | bytes 786464 | tf_op jit(solution)/shard_map/ppermute | solution.py:95
  48.8 64.5 %collective-permute-done.3 = bf16[256,3072]{1,0:T(8,128)(2,1)} collective-permute-done((bf16[256,3072]{1,0:T(8,128)(2,1)S(1)}, bf16[256,3072]{1,0:T(8,128)(2,1)}, u32[]{:S(2)}, u32[]{:S(2)}) %collective-permute-start.3) | collective-permute-done | bytes 1572896 | tf_op jit(solution)/shard_map/ppermute | solution.py:95
  120.1 183.3 %collective-permute-done.4 = bf16[512,3072]{1,0:T(8,128)(2,1)} collective-permute-done((bf16[512,3072]{1,0:T(8,128)(2,1)S(1)}, bf16[512,3072]{1,0:T(8,128)(2,1)}, u32[]{:S(2)}, u32[]{:S(2)}) %collective-permute-start.4) | collective-permute-done | bytes 3145760 | tf_op jit(solution)/shard_map/ppermute | solution.py:95
  303.5 5.6 maximum_select_fusion
  314.4 3.8 fusion.33
  331.6 3.8 fusion.177
  361.2 5.7 multiply_convert_fusion.4
  371.0 27.5 %all-gather.5.cloned.1.call-done = bf16[1536,3072]{1,0:T(8,128)(2,1)} async-done(((bf16[96,3072]{1,0:T(8,128)(2,1)}), bf16[1536,3072]{1,0:T(8,128)(2,1)}) %all-gather.5.cloned.1.call-update) | async-done | bytes 9437200 | tf_op jit(solution)/shard_map/all_gather | solution.py:109
  398.5 6.2 fusion.9
  406.5 3.8 multiply_convert_fusion.1
  411.7 4.9 fusion.30
  422.2 4.6 fusion.23
  431.9 4.6 fusion.16
  438.7 4.4 pad_maximum_fusion
  443.1 4.4 pad_maximum_fusion.1
  447.5 12.6 %copy.130 = bf16[1536,3072]{1,0:T(8,128)(2,1)} copy(bf16[1536,3072]{0,1:T(8,128)(2,1)} %pad_maximum_fusion) | data formatting | bytes 18874368
  460.2 12.7 %copy.132 = bf16[1536,3072]{1,0:T(8,128)(2,1)} copy(bf16[1536,3072]{0,1:T(8,128)(2,1)} %pad_maximum_fusion.1) | data formatting | bytes 18874368
  474.1 3.7 fusion.53
  477.8 4.2 fusion.47
  550.3 5.2 fusion.169
  565.4 64.2 %reduce-scatter.10.cloned.1.call-done = bf16[96,3072]{1,0:T(8,128)(2,1)} async-done(((bf16[1536,3072]{1,0:T(8,128)(2,1)}), bf16[96,3072]{1,0:T(8,128)(2,1)}) %reduce-scatter.10.cloned.1.call-update) | async-done | bytes 589840
  631.9 174.4 %reduce-scatter.12.cloned.1.call-done = bf16[96,3072]{1,0:T(8,128)(2,1)} async-done(((bf16[1536,3072]{1,0:T(8,128)(2,1)}), bf16[96,3072]{1,0:T(8,128)(2,1)}) %reduce-scatter.12.cloned.1.call-update) | async-done | bytes 589840
  817.1 108.2 %reduce-scatter.8.cloned.1.call-done = bf16[32,3072]{1,0:T(8,128)(2,1)} async-done(((bf16[1024,3072]{1,0:T(8,128)(2,1)}), bf16[32,3072]{1,0:T(8,128)(2,1)}) %reduce-scatter.8.cloned.1.call-update) | async-done | bytes 196624 | tf_op jit(solution)/shard_map/reduce_scatter | solution.py:298
  (482 shorter events, 182.3 us)
Async XLA Ops:
  7.3 353.9 %all-gather.3.cloned.1.call-start = ((), (), s32[]{:S(2)}) async-start(), calls=%async_computation.3 | async-start | bytes 10027008 | tf_op jit(solution)/shard_map/all_gather | solution.py:102
  9.4 389.1 %all-gather.5.cloned.1.call-start = ((), (), s32[]{:S(2)}) async-start(), calls=%async_computation.4 | async-start | bytes 10027008 | tf_op jit(solution)/shard_map/all_gather | solution.py:109
  11.4 618.2 %reduce-scatter.10.cloned.1.call-start = ((), (), s32[]{:S(2)}) async-start(), calls=%async_computation.6 | async-start | bytes 10027008
  12.0 1.6 collective-permute-start
  13.7 14.2 %collective-permute-start.1 = (bf16[64,3072]{1,0:T(8,128)(2,1)S(1)}, bf16[64,3072]{1,0:T(8,128)(2,1)S(1)}, u32[]{:S(2)}, u32[]{:S(2)}) collective-permute-start(bf16[64,3072]{1,0:T(8,128)(2,1)S(1)} %maximum_select_fusion.4), channel_id=1, source_target_pairs={{0,2},{1,3},{2,0},{3,1},{4,6},{5,7},{6,4},{7,5},{8,10},{9,11},{10,... | collective-permute-start | bytes 1179656 | tf_op jit(solution)/shard_map/ppermute | solution.py:95
  28.1 18.8 %collective-permute-start.2 = (bf16[128,3072]{1,0:T(8,128)(2,1)S(1)}, bf16[128,3072]{1,0:T(8,128)(2,1)S(1)}, u32[]{:S(2)}, u32[]{:S(2)}) collective-permute-start(bf16[128,3072]{1,0:T(8,128)(2,1)S(1)} %maximum_select_fusion.3), channel_id=1, source_target_pairs={{0,4},{1,5},{2,6},{3,7},{4,0},{5,1},{6,2},{7,3},{8,12},{9,13},{10,... | collective-permute-start | bytes 2359304 | tf_op jit(solution)/shard_map/ppermute | solution.py:95
  47.2 66.0 %collective-permute-start.3 = (bf16[256,3072]{1,0:T(8,128)(2,1)S(1)}, bf16[256,3072]{1,0:T(8,128)(2,1)}, u32[]{:S(2)}, u32[]{:S(2)}) collective-permute-start(bf16[256,3072]{1,0:T(8,128)(2,1)S(1)} %maximum_select_fusion.2), channel_id=1, source_target_pairs={{0,8},{1,9},{2,10},{3,11},{4,12},{5,13},{6,14},{7,15},{8,0},{9,1},... | collective-permute-start | bytes 4718600 | tf_op jit(solution)/shard_map/ppermute | solution.py:95
  48.8 70.7 %copy-start.98 = (s32[394,2]{0,1:T(2,128)S(1)}, s32[394,2]{0,1:T(2,128)}, u32[]{:S(2)}) copy-start(s32[394,2]{0,1:T(2,128)} %param.30) | copy-start | bytes 9460
  116.7 186.7 %collective-permute-start.4 = (bf16[512,3072]{1,0:T(8,128)(2,1)S(1)}, bf16[512,3072]{1,0:T(8,128)(2,1)}, u32[]{:S(2)}, u32[]{:S(2)}) collective-permute-start(bf16[512,3072]{1,0:T(8,128)(2,1)S(1)} %maximum_select_fusion.1), channel_id=1, source_target_pairs={{0,16},{1,17},{2,18},{3,19},{4,20},{5,21},{6,22},{7,23},{8,24},{9,... | collective-permute-start | bytes 9437192 | tf_op jit(solution)/shard_map/ppermute | solution.py:95
  118.1 196.3 %copy-start.80 = (f32[394]{0:T(512)}, f32[394]{0:T(512)S(1)}, u32[]{:S(2)}) copy-start(f32[394]{0:T(512)S(1)} %broadcast_multiply_fusion.1) | copy-start | bytes 4732
  119.5 194.9 %copy-start.96 = (f32[394]{0:T(512)}, f32[394]{0:T(512)S(1)}, u32[]{:S(2)}) copy-start(f32[394]{0:T(512)S(1)} %fusion.142) | copy-start | bytes 4732
  313.4 30.0 %copy-start.82 = (bf16[1,768]{1,0:T(2,128)(2,1)}, bf16[1,768]{1,0:T(2,128)(2,1)S(1)}, u32[]{:S(2)}) copy-start(bf16[1,768]{1,0:T(2,128)(2,1)S(1)} %stack_reshape.15) | copy-start | bytes 4612
  313.5 29.9 %copy-start.84 = (bf16[1,768]{1,0:T(2,128)(2,1)}, bf16[1,768]{1,0:T(2,128)(2,1)S(1)}, u32[]{:S(2)}) copy-start(bf16[1,768]{1,0:T(2,128)(2,1)S(1)} %stack_reshape.14) | copy-start | bytes 4612
  313.6 29.8 %copy-start.86 = (bf16[1,768]{1,0:T(2,128)(2,1)}, bf16[1,768]{1,0:T(2,128)(2,1)S(1)}, u32[]{:S(2)}) copy-start(bf16[1,768]{1,0:T(2,128)(2,1)S(1)} %stack_reshape.13) | copy-start | bytes 4612
  342.8 175.8 %copy-start = (f32[394,768]{1,0:T(8,128)}, f32[394,768]{1,0:T(8,128)S(1)}, u32[]{:S(2)}) copy-start(f32[394,768]{1,0:T(8,128)S(1)} %get-tuple-element.184) | copy-start | bytes 3631108
  344.1 167.5 %copy-start.63 = (f32[394,4]{0,1:T(4,128)}, f32[394,4]{0,1:T(4,128)S(1)}, u32[]{:S(2)}) copy-start(f32[394,4]{0,1:T(4,128)S(1)} %get-tuple-element.124) | copy-start | bytes 18916
  344.1 170.7 %copy-start.101 = (s32[394,1]{0,1:T(1,128)}, s32[394,1]{0,1:T(1,128)S(1)}, u32[]{:S(2)}) copy-start(s32[394,1]{0,1:T(1,128)S(1)} %get-tuple-element.177) | copy-start | bytes 4732
  344.1 170.7 %copy-start.103 = (s32[394,1]{0,1:T(1,128)}, s32[394,1]{0,1:T(1,128)S(1)}, u32[]{:S(2)}) copy-start(s32[394,1]{0,1:T(1,128)S(1)} %get-tuple-element.178) | copy-start | bytes 4732
  347.0 9.1 collective-permute-start.6
  349.5 9.1 collective-permute-start.5
  460.2 346.1 %reduce-scatter.12.cloned.1.call-start = ((), (), s32[]{:S(2)}) async-start(), calls=%async_computation.7 | async-start | bytes 10027008
  472.9 452.4 %reduce-scatter.8.cloned.1.call-start = ((), (), s32[]{:S(2)}) async-start(), calls=%async_computation.5 | async-start | bytes 6488064 | tf_op jit(solution)/shard_map/reduce_scatter | solution.py:298
  487.1 19.9 %collective-permute-start.7 = (bf16[4,256,768]{2,1,0:T(8,128)(2,1)}, bf16[4,256,768]{2,1,0:T(8,128)(2,1)}, u32[]{:S(2)}, u32[]{:S(2)}) collective-permute-start(bf16[4,256,768]{2,1,0:T(8,128)(2,1)} %pad_maximum_fusion.3), channel_id=1, source_target_pairs={{0,1},{1,0},{2,3},{3,2},{4,5},{5,4},{6,7},{7,6},{8,9},{9,8},{10,11... | collective-permute-start | bytes 4718600 | tf_op jit(solution)/shard_map/ppermute | solution.py:173
  506.1 6.0 collective-permute-start.8
  (124 other events, 447.9 us)
Sparse Core Ops, SparseCore 0:
  11.5 230.4 all-gather.2
  245.4 153.0 all-gather.4
  460.3 169.2 reduce-scatter.9
  636.1 170.1 reduce-scatter.11
  811.7 113.5 reduce-scatter.7
